TPU v7x, 32 devices: a whole 2x2x4 slice. The times are simulated.
32 devices in a mesh: fsdp: 16 (over z, y, core), tp: 2 (over x).
Axes of the slice: x: 2, y: 2, z: 4, core: 2. Of those that a mesh axis runs over, the one named last changes fastest.
Arguments:
- hidden: bfloat16 [16384, 2048], P(('fsdp', 'tp')), may hold values from -6 to 6
- cotangent: bfloat16 [16384, 2048], P(('fsdp', 'tp')), may hold values from -6 to 6
- prefix: int32 [16], P('fsdp'), may hold values from 102 to 512, as said below
- input_norm_gain: bfloat16 [2048], P('fsdp'), may hold values from 0.5 to 1.5
- z_weight: bfloat16 [2048, 4096], P('fsdp', 'tp'), may hold values from -0.125 to 0.125
- x_weight: bfloat16 [2048, 4096], P('fsdp', 'tp'), may hold values from -0.125 to 0.125
- bc_weight: bfloat16 [2048, 256], P('fsdp'), may hold values from -0.125 to 0.125
- dt_weight: bfloat16 [2048, 64], P('fsdp', 'tp'), may hold values from -0.125 to 0.125
- x_conv: bfloat16 [64, 4, 64], P('tp', None, 'fsdp'), may hold values from -3 to 3
- bc_conv: bfloat16 [4, 256], P(None, 'fsdp'), may hold values from -3 to 3
- log_decay: float32 [64], P('tp'), may hold values from 0 to 2.77
- dt_bias: float32 [64], P('tp'), may hold values from -4 to -1
- skip_gain: float32 [64], P('tp'), may hold values from 0.5 to 1.5
- gate_gain: bfloat16 [64, 64], P('tp', 'fsdp'), may hold values from 0.5 to 1.5
- out_weight: bfloat16 [4096, 2048], P('tp', 'fsdp'), may hold values from -0.09375 to 0.09375
Outputs:
- mixed: float32 [16384, 2048], P(('fsdp', 'tp'))
- grad_hidden: float32 [16384, 2048], P(('fsdp', 'tp'))
- grad_input_norm_gain: float32 [2048], P('fsdp')
- grad_z_weight: float32 [2048, 4096], P('fsdp', 'tp')
- grad_x_weight: float32 [2048, 4096], P('fsdp', 'tp')
- grad_bc_weight: float32 [2048, 256], P('fsdp')
- grad_dt_weight: float32 [2048, 64], P('fsdp', 'tp')
- grad_x_conv: float32 [64, 4, 64], P('tp', None, 'fsdp')
- grad_bc_conv: float32 [4, 256], P(None, 'fsdp')
- grad_log_decay: float32 [64], P('tp')
- grad_dt_bias: float32 [64], P('tp')
- grad_skip_gain: float32 [64], P('tp')
- grad_gate_gain: float32 [64, 64], P('tp', 'fsdp')
- grad_out_weight: float32 [4096, 2048], P('tp', 'fsdp')
Inputs may be any that keep to these rules, and one draw needn't show every extreme that they name: `prefix`: prefix length of each sequence; some sequence has the least and some the most.
All inputs are finite; a program needn't handle non-finite values.
Results may differ from a plain program's by a relative error of at most 0.0082.
Values may be sent and summed in bfloat16 or wider, within the bound.
No kernel may reach another device: no remote copies, remote signals or barrier semaphores. Data moves between devices by JAX's collectives and lax.ppermute only.
A program may use at most 384 MiB of HBM per device.

v0:
```python
import jax
import jax.numpy as jnp
from jax import lax
from jax.sharding import PartitionSpec as P

H = 64
P_SIZE = 64
Q = 256


EPSILON = 1e-05
HIGHEST = lax.Precision.HIGHEST


def causal_conv(values, kernel):
    kernel_len = kernel.shape[0]
    length = values.shape[1]
    padded = jnp.pad(values, ((0, 0), (kernel_len - 1, 0), (0, 0)))
    running = kernel[0] * padded[:, 0:length]
    for offset in range(1, kernel_len):
        running = running + kernel[offset] * padded[:, offset : offset + length]
    return running


def block_scan(inputs, steps_dt, rates, b_mat, c_mat, block_len):
    seq_count, length, head_count, head_width = inputs.shape
    block_count = length // block_len
    inputs = inputs.reshape(seq_count, block_count, block_len, head_count, head_width)
    steps_dt = steps_dt.reshape(seq_count, block_count, block_len, head_count)
    rates = rates.reshape(seq_count, block_count, block_len, head_count)
    b_mat = b_mat.reshape(seq_count, block_count, block_len, -1)
    c_mat = c_mat.reshape(seq_count, block_count, block_len, -1)
    cumulative = jnp.cumsum(rates, axis=2)
    products = jnp.einsum("scqn,sckn->scqk", c_mat, b_mat, precision=HIGHEST)
    exponent = cumulative[:, :, :, None, :] - cumulative[:, :, None, :, :]
    causal_mask = (jnp.arange(block_len)[:, None] >= jnp.arange(block_len)[None, :])[
        None, None, :, :, None
    ]
    decays = jnp.where(causal_mask, jnp.exp(jnp.where(causal_mask, exponent, 0.0)), 0.0)
    mixing = products[..., None] * decays * steps_dt[:, :, None, :, :]
    local_out = jnp.einsum("sctkh,sckhp->scthp", mixing, inputs, precision=HIGHEST)
    last_cum = cumulative[:, :, -1:, :]
    to_last = jnp.exp(last_cum - cumulative) * steps_dt
    states = jnp.einsum("sckh,sckhp,sckn->schpn", to_last, inputs, b_mat, precision=HIGHEST)
    growth = jnp.exp(last_cum[:, :, 0, :])

    def advance(current, element):
        block_state, factor = element
        return (current * factor[:, :, None, None] + block_state, current)

    initial = jnp.zeros(states.shape[:1] + states.shape[2:], inputs.dtype)
    _, entering = lax.scan(
        advance, initial, (jnp.moveaxis(states, 1, 0), jnp.moveaxis(growth, 1, 0))
    )
    entering = jnp.moveaxis(entering, 0, 1)
    carried = (
        jnp.einsum("sctn,schpn->scthp", c_mat, entering, precision=HIGHEST)
        * jnp.exp(cumulative)[..., None]
    )
    return (local_out + carried).reshape(seq_count, length, head_count, head_width)


def mixer(x_pre, bc_pre, dt_pre, x_conv, bc_conv, log_decay, dt_bias, skip_gain, prefix, block_len):
    head_count, kernel_len, head_width = x_conv.shape
    seq_count, length = (x_pre.shape[0], x_pre.shape[1])
    x_kernel = jnp.transpose(x_conv, (1, 0, 2)).reshape(kernel_len, head_count * head_width)
    inputs = jax.nn.silu(causal_conv(x_pre, x_kernel)).reshape(
        seq_count, length, head_count, head_width
    )
    bc_act = jax.nn.silu(causal_conv(bc_pre, bc_conv))
    state_len = bc_pre.shape[-1] // 2
    b_mat = bc_act[..., :state_len]
    c_mat = bc_act[..., state_len:]
    steps_dt = jax.nn.softplus(dt_pre + dt_bias)
    rates = -jnp.exp(log_decay) * steps_dt
    prefix_mask = (jnp.arange(length)[None, :] < prefix[:, None]).astype(inputs.dtype)
    masked = inputs * prefix_mask[:, :, None, None]
    forward_out = block_scan(inputs, steps_dt, rates, b_mat, c_mat, block_len)
    flipped = block_scan(
        jnp.flip(masked, 1),
        jnp.flip(steps_dt, 1),
        jnp.flip(rates, 1),
        jnp.flip(b_mat, 1),
        jnp.flip(c_mat, 1),
        block_len,
    )
    diagonal = jnp.sum(b_mat * c_mat, axis=-1)[:, :, None, None] * steps_dt[..., None] * masked
    result = forward_out + jnp.flip(flipped, 1) - diagonal + skip_gain[:, None] * inputs
    return result.reshape(seq_count, length, head_count * head_width)


def on_device(
    hidden,
    cotangent,
    prefix,
    input_norm_gain,
    z_weight,
    x_weight,
    bc_weight,
    dt_weight,
    x_conv,
    bc_conv,
    log_decay,
    dt_bias,
    skip_gain,
    gate_gain,
    out_weight,
):
    gathered = (
        lax.all_gather(input_norm_gain, "fsdp", axis=0, tiled=True),
        lax.all_gather(z_weight, "fsdp", axis=0, tiled=True),
        lax.all_gather(x_weight, "fsdp", axis=0, tiled=True),
        lax.all_gather(bc_weight, "fsdp", axis=0, tiled=True),
        lax.all_gather(dt_weight, "fsdp", axis=0, tiled=True),
        lax.all_gather(x_conv, "fsdp", axis=2, tiled=True),
        lax.all_gather(bc_conv, "fsdp", axis=1, tiled=True),
        lax.all_gather(gate_gain, "fsdp", axis=1, tiled=True),
        lax.all_gather(out_weight, "fsdp", axis=1, tiled=True),
    )
    hidden_wide = hidden.astype(jnp.float32)
    inv_rms = lax.rsqrt(jnp.mean(hidden_wide * hidden_wide, axis=-1, keepdims=True) + EPSILON)
    norm_full = gathered[0].astype(jnp.float32)
    normed = (hidden_wide * inv_rms * norm_full).astype(jnp.bfloat16)
    normed_all = lax.all_gather(normed, "tp", axis=0, tiled=True)
    gate_pre = jnp.dot(normed_all, gathered[1], preferred_element_type=jnp.float32)
    x_pre = jnp.dot(normed_all, gathered[2], preferred_element_type=jnp.float32)
    bc_pre = jnp.dot(normed_all, gathered[3], preferred_element_type=jnp.float32)
    dt_pre = jnp.dot(normed_all, gathered[4], preferred_element_type=jnp.float32)
    token_count = normed_all.shape[0]
    seq_count = prefix.shape[0]
    length = token_count // seq_count

    def local_mix(x_in, bc_in, dt_in, x_taps, bc_taps, decay_log, bias_dt, gain_skip):
        result = mixer(
            x_in.reshape(seq_count, length, -1),
            bc_in.reshape(seq_count, length, -1),
            dt_in.reshape(seq_count, length, -1),
            x_taps,
            bc_taps,
            decay_log,
            bias_dt,
            gain_skip,
            prefix,
            Q,
        )
        return result.reshape(token_count, -1)

    ssd_out, mixer_back = jax.vjp(
        local_mix,
        x_pre,
        bc_pre,
        dt_pre,
        gathered[5].astype(jnp.float32),
        gathered[6].astype(jnp.float32),
        log_decay,
        dt_bias,
        skip_gain,
    )
    gate_act = jax.nn.silu(gate_pre)
    gated = ssd_out * gate_act
    square_sum = lax.psum(jnp.sum(gated * gated, axis=-1), "tp")
    inv_gate = lax.rsqrt(square_sum / (H * P_SIZE) + EPSILON)[:, None]
    gate_full = gathered[7].reshape(-1).astype(jnp.float32)
    projected = (gated * inv_gate * gate_full).astype(jnp.bfloat16)
    out_full = gathered[8]
    branch = lax.psum_scatter(
        jnp.dot(projected, out_full, preferred_element_type=jnp.float32),
        "tp",
        scatter_dimension=0,
        tiled=True,
    )
    mixed = hidden_wide + branch
    cot_all = lax.all_gather(cotangent, "tp", axis=0, tiled=True)
    grad_out_weight = jnp.einsum(
        "tc,td->cd", projected, cot_all, preferred_element_type=jnp.float32
    )
    grad_projected = jnp.einsum(
        "td,cd->tc", cot_all, gathered[8], preferred_element_type=jnp.float32
    )
    grad_gate_gain = jnp.sum(grad_projected * gated * inv_gate, axis=0).reshape(gathered[7].shape)
    scaled = grad_projected * gathered[7].reshape(-1).astype(jnp.float32)
    dot_sum = lax.psum(jnp.sum(scaled * gated, axis=-1), "tp")
    grad_gated = (
        inv_gate * scaled
        - gated * inv_gate * inv_gate * inv_gate * (dot_sum / (H * P_SIZE))[:, None]
    )
    grad_ssd = grad_gated * gate_act
    sigma = jax.nn.sigmoid(gate_pre)
    grad_gate_pre = (grad_gated * ssd_out * sigma * (1.0 + gate_pre * (1.0 - sigma))).astype(
        jnp.bfloat16
    )
    (
        grad_x_pre,
        grad_bc_pre,
        grad_dt_pre,
        grad_x_conv,
        grad_bc_conv,
        grad_log_decay,
        grad_dt_bias,
        grad_skip_gain,
    ) = mixer_back(grad_ssd)
    grad_x_low = grad_x_pre.astype(jnp.bfloat16)
    grad_dt_low = grad_dt_pre.astype(jnp.bfloat16)
    partial_normed = jnp.einsum(
        "tc,dc->td", grad_gate_pre, gathered[1], preferred_element_type=jnp.float32
    )
    partial_normed = partial_normed + jnp.einsum(
        "tc,dc->td", grad_x_low, gathered[2], preferred_element_type=jnp.float32
    )
    partial_normed = partial_normed + jnp.einsum(
        "tc,dc->td", grad_dt_low, gathered[4], preferred_element_type=jnp.float32
    )
    grad_normed, grad_bc_own = (
        lax.psum_scatter(partial_normed, "tp", scatter_dimension=0, tiled=True),
        lax.psum_scatter(grad_bc_pre, "tp", scatter_dimension=0, tiled=True),
    )
    grad_bc_low = grad_bc_own.astype(jnp.bfloat16)
    grad_normed = grad_normed + jnp.einsum(
        "tc,dc->td", grad_bc_low, gathered[3], preferred_element_type=jnp.float32
    )
    grad_z_weight = jnp.einsum(
        "td,tc->dc", normed_all, grad_gate_pre, preferred_element_type=jnp.float32
    )
    grad_x_weight = jnp.einsum(
        "td,tc->dc", normed_all, grad_x_low, preferred_element_type=jnp.float32
    )
    grad_dt_weight = jnp.einsum(
        "td,tc->dc", normed_all, grad_dt_low, preferred_element_type=jnp.float32
    )
    grad_bc_weight = jnp.einsum(
        "td,tc->dc", normed, grad_bc_low, preferred_element_type=jnp.float32
    )
    back_norm = gathered[0].astype(jnp.float32)
    grad_norm_gain = jnp.sum(grad_normed * hidden_wide * inv_rms, axis=0)
    scaled_in = grad_normed * back_norm
    grad_hidden = (
        inv_rms * scaled_in
        - hidden_wide
        * inv_rms
        * inv_rms
        * inv_rms
        * jnp.mean(scaled_in * hidden_wide, axis=-1, keepdims=True)
        + cotangent.astype(jnp.float32)
    )
    norm_part, z_part, x_part, bc_part, dt_part, xconv_part, bcconv_part, gain_part, out_part = (
        lax.psum_scatter(grad_norm_gain, "fsdp", scatter_dimension=0, tiled=True),
        lax.psum_scatter(grad_z_weight, "fsdp", scatter_dimension=0, tiled=True),
        lax.psum_scatter(grad_x_weight, "fsdp", scatter_dimension=0, tiled=True),
        lax.psum_scatter(grad_bc_weight, "fsdp", scatter_dimension=0, tiled=True),
        lax.psum_scatter(grad_dt_weight, "fsdp", scatter_dimension=0, tiled=True),
        lax.psum_scatter(grad_x_conv, "fsdp", scatter_dimension=2, tiled=True),
        lax.psum_scatter(grad_bc_conv, "fsdp", scatter_dimension=1, tiled=True),
        lax.psum_scatter(grad_gate_gain, "fsdp", scatter_dimension=1, tiled=True),
        lax.psum_scatter(grad_out_weight, "fsdp", scatter_dimension=1, tiled=True),
    )
    shared_norm, shared_bc, shared_conv = lax.psum((norm_part, bc_part, bcconv_part), "tp")
    head_decay, head_bias, head_skip = lax.psum(
        (grad_log_decay, grad_dt_bias, grad_skip_gain), "fsdp"
    )
    return (
        mixed,
        grad_hidden,
        shared_norm,
        z_part,
        x_part,
        shared_bc,
        dt_part,
        xconv_part,
        shared_conv,
        head_decay,
        head_bias,
        head_skip,
        gain_part,
        out_part,
    )


def solution(mesh):
    return jax.shard_map(
        on_device,
        mesh=mesh,
        in_specs=(
            P(("fsdp", "tp"), None),
            P(("fsdp", "tp"), None),
            P("fsdp"),
            P("fsdp"),
            P("fsdp", "tp"),
            P("fsdp", "tp"),
            P("fsdp", None),
            P("fsdp", "tp"),
            P("tp", None, "fsdp"),
            P(None, "fsdp"),
            P("tp"),
            P("tp"),
            P("tp"),
            P("tp", "fsdp"),
            P("tp", "fsdp"),
        ),
        out_specs=(
            P(("fsdp", "tp"), None),
            P(("fsdp", "tp"), None),
            P("fsdp"),
            P("fsdp", "tp"),
            P("fsdp", "tp"),
            P("fsdp", None),
            P("fsdp", "tp"),
            P("tp", None, "fsdp"),
            P(None, "fsdp"),
            P("tp"),
            P("tp"),
            P("tp"),
            P("tp", "fsdp"),
            P("tp", "fsdp"),
        ),
        check_vma=False,
    )
```

profile of v0, /device:TPU:0, one launch (start us, length us, event | category | flops | bytes accessed | tf_op | source)
XLA Modules:
  0.0 2084.8 jit_solution(17103307356082759630)
XLA Ops:
  8.0 23.2 %all-gather = bf16[16,1,128]{2,1,0:T(2,128)(2,1)S(1)} all-gather(bf16[1,1,128]{2,1,0:T(2,128)(2,1)} %bitcast.676), channel_id=1, replica_groups=mesh['fsdp'=16,'tp'=2] {'fsdp'}, dimensions={0}, use_global_device_ids=true | all-gather | bytes 4352 | tf_op jit(solution)/shard_map/all_gather | solution.py:110
  42.3 17.4 all-gather.1
  59.8 18.9 all-gather.2
  79.5 17.6 all_gather.33
  99.0 19.2 all_gather.39
  213.5 21.0 %fusion.51 = (f32[1,1024,2048]{2,1,0:T(8,128)}, f32[1,1024,2048]{2,1,0:T(8,128)}) fusion(f32[1024,2048]{1,0:T(8,128)} %fusion.209, f32[2048]{0:T(1024)S(1)} %mul.856, f32[2048]{0:T(1024)S(1)} %copy-done.77, f32[2048]{0:T(1024)S(1)} %copy-done.79, f32[1,1024,2048]{2,1,0:T(8,128)} %bitcast.592, f32[2048]{0:T(1024)S(1)} %mul.842), kind=kLoop, calls=%fused_computation.111 | loop fusion | flops 23068672 | bytes 33587200 | tf_op jit(solution)/shard_map/jvp(jit(silu))/mul | solution.py:67
  292.3 45.4 %fusion.48 = f32[1,4,32,8,8,256]{5,4,3,2,1,0:T(8,128)} fusion(f32[4,256,32,64]{1,3,2,0:T(8,128)S(1)} %fusion.100, f32[4,256,32]{1,2,0:T(8,128)S(1)} %copy-done.49, f32[4,256,32]{1,2,0:T(8,128)S(1)} %copy-done.69, f32[4,256,32]{1,2,0:T(8,128)S(1)} %copy-done.64, f32[4,256,256]{2,1,0:T(8,128)S(1)} %copy-done.56, pred[256,256]{1,0:T(8,128)(4,1)S(1)} %copy-done.81, ...), kind=kOutput, calls=%fused_computation.86 | convolution fusion | flops 6488588288 | bytes 26673152 | tf_op jit(solution)/shard_map/jvp(sctkh,sckhp->scthp)/dot_general | solution.py:41
  414.9 40.7 %fusion.47 = f32[1,4,32,8,8,256]{5,4,3,2,1,0:T(8,128)S(1)} fusion(f32[4,256,32,64]{1,3,2,0:T(8,128)S(1)} %fusion.97, f32[4,256,32]{1,2,0:T(8,128)S(1)} %copy-done.48, f32[4,256,32]{1,2,0:T(8,128)S(1)} %copy-done.66, f32[4,256,32]{1,2,0:T(8,128)S(1)} %copy-done.62, f32[4,256,256]{2,1,0:T(8,128)S(1)} %copy-done.54, pred[256,256]{1,0:T(8,128)(4,1)S(1)} %copy-done.82, ...), kind=kOutput, calls=%fused_computation.84 | convolution fusion | flops 6488588288 | bytes 26673152 | tf_op jit(solution)/shard_map/jvp(sctkh,sckhp->scthp)/dot_general | solution.py:41
  495.8 17.7 multiply_reduce_fusion.13
  518.5 16.8 multiply_reduce_fusion.4
  540.2 21.6 %fusion.49 = (f32[2048]{0:T(1024)}, f32[1024,2048]{1,0:T(8,128)}, bf16[1024,2048]{1,0:T(8,128)(2,1)}) fusion(f32[1,1024,2048]{2,1,0:T(8,128)} %get-tuple-element.865, f32[1024,2048]{1,0:T(8,128)} %get-tuple-element.911, f32[1024]{0:T(1024)S(1)} %broadcast_multiply_fusion.11, f32[1024,2048]{1,0:T(8,128)} %get-tuple-element.859, ...), kind=kLoop, calls=%fused_computation.88 | loop fusion | flops 52426752 | bytes 54550528 | tf_op jit(solution)/shard_map/transpose(jvp())/reduce_sum | solution.py:88
  591.2 14.7 fusion.137
  721.9 14.7 multiply_reduce_fusion.3
  736.6 34.5 %fusion.45 = f32[1,4,32,8,8,256]{5,4,3,2,1,0:T(8,128)} fusion(f32[4,256,32,64]{1,3,2,0:T(8,128)} %fusion.122, f32[4,256,32]{1,2,0:T(8,128)S(1)} %copy-done.43, f32[4,256,32]{1,2,0:T(8,128)S(1)} %copy-done.67, f32[4,256,32]{1,2,0:T(8,128)S(1)} %copy-done.63, f32[4,256,256]{2,1,0:T(8,128)} %fusion.212, pred[256,256]{1,0:T(8,128)(4,1)S(1)} %copy-done.83, ...), kind=kOutput, calls=%fused_computation.80 | convolution fusion | flops 6488588288 | bytes 26673152 | tf_op jit(solution)/shard_map/transpose(jvp(sctkh,sckhp->scthp))/dot_general | solution.py:41
  771.1 33.1 %fusion.52 = f32[4,32,256,256]{3,2,1,0:T(8,128)} fusion(f32[4,32,64,256]{3,0,2,1:T(4,128)} %bitcast.599, f32[4,256,32,64]{1,0,3,2:T(4,128)S(1)} %bitcast.591), kind=kOutput, calls=%fused_computation.117 | convolution fusion | flops 6442450944 | bytes 50331648 | tf_op jit(solution)/shard_map/transpose(jvp(sctkh,sckhp->scthp))/dot_general | solution.py:41
  807.7 23.1 %while.70 = (s32[]{:T(128)}, f32[1,32,64,128]{3,2,1,0:T(8,128)}, f32[4,1,32,64,128]{4,3,2,1,0:T(8,128)}, f32[4,1,32]{2,1,0:T(1,128)S(1)}, f32[4,1,32,64,128]{4,3...) while((s32[]{:T(128)}, f32[1,32,64,128]{3,2,1,0:T(8,128)}, ...), condition=%wide.region_17.18_spmd.clone, body=%wide.region_15.17_spmd.clone.sunk | while | flops 1572836 | bytes 6293140 | solution.py:52
  880.4 33.6 %fusion.46 = f32[1,4,32,8,8,256]{5,4,3,2,1,0:T(8,128)S(1)} fusion(f32[4,256,32,64]{1,3,2,0:T(8,128)} %fusion.119, f32[4,256,32]{1,2,0:T(8,128)S(1)} %copy-done.46, f32[4,256,32]{1,2,0:T(8,128)S(1)} %copy-done.70, f32[4,256,32]{1,2,0:T(8,128)S(1)} %copy-done.65, f32[4,256,256]{2,1,0:T(8,128)S(1)} %copy-done.57, pred[256,256]{1,0:T(8,128)(4,1)S(1)} %copy-done.83, ...), kind=kOutput, calls=%fused_computation.82 | convolution fusion | flops 6488588288 | bytes 26673152 | tf_op jit(solution)/shard_map/transpose(jvp(sctkh,sckhp->scthp))/dot_general | solution.py:41
  918.4 22.0 %multiply_reduce_fusion.11 = (f32[1024,32]{0,1:T(8,128)}, f32[1,1024,32,64]{1,3,2,0:T(8,128)}) fusion(f32[1,1024,32,64]{1,3,2,0:T(8,128)} %bitcast.586, f32[1,1024,32,64]{1,3,2,0:T(8,128)} %bitcast.587, f32[1024]{0:T(1024)S(1)} %copy-done.85, f32[1,1024,32,64]{1,3,2,0:T(8,128)} %rev.43, f32[1024,32]{0,1:T(8,128)S(1)} %copy-done.40, ...), kind=kLoop, calls=%fused_computation.99 | loop fusion | flops 23035904 | bytes 50598016 | tf_op jit(solution)/shard_map/transpose(jvp())/reduce_sum | solution.py:87
  949.7 70.0 %fusion.17 = (f32[4,256,32]{1,2,0:T(8,128)}, f32[4,256,32]{1,2,0:T(8,128)}, f32[4,256,32]{1,2,0:T(8,128)}, f32[4,256,256]{2,1,0:T(8,128)S(1)}, f32[4,256,256]{2,...) fusion(f32[4,256,32]{1,2,0:T(8,128)S(1)} %copy-done.70, ...), kind=kOutput, calls=%fused_computation.47 | convolution fusion | flops 6693388288 | bytes 55902208 | tf_op jit(solution)/shard_map/transpose(jvp(sctkh,sckhp->scthp))/dot_general | solution.py:41
  1128.2 19.3 multiply_reduce_fusion.7
  1202.4 16.0 fusion.200
  1223.0 16.2 fusion.199
  1239.3 15.5 fusion.215
  1254.8 15.2 fusion.216
  1274.0 71.0 %reduce-scatter.15.cloned.1.call-done = f32[512,2048]{1,0:T(8,128)} async-done(((f32[1024,2048]{1,0:T(8,128)}), f32[512,2048]{1,0:T(8,128)}) %reduce-scatter.15.cloned.1.call-update) | async-done | bytes 4194320 | tf_op jit(solution)/shard_map/reduce_scatter | solution.py:214
  1350.9 62.9 %all-reduce.25 = (f32[2048]{0:T(1024)S(1)}, f32[32,4,64]{0,1,2:T(4,128)S(1)}, f32[32]{0:T(128)}, f32[32]{0:T(128)}, f32[32]{0:T(128)}, /*index=5*/f32[32,64]{1,0:T(8,128)S(1)}) all-reduce(f32[2048]{0:T(1024)S(1)} %get-tuple-element.782, f32[32,4,64]{0,1,2:T(4,128)S(1)} %copy.684, ...), channel_id=5, replica_groups=mesh['fsdp'=16,'tp'=2] {'fsdp'}, use_global_device_ids=true, to_apply=%region_43.44.clone | all-reduce | flops 12384 | bytes 99072
  1420.8 26.0 %reduce-scatter.13.cloned.1.call-done = f32[512,2048]{1,0:T(8,128)} async-done(((f32[1024,2048]{1,0:T(8,128)}), f32[512,2048]{1,0:T(8,128)}) %reduce-scatter.13.cloned.1.call-update) | async-done | bytes 4194320 | tf_op jit(solution)/shard_map/reduce_scatter | solution.py:166
  1453.9 52.2 %reduce-scatter.25.cloned.1.call-done = f32[128,32]{0,1:T(8,128)} async-done(((f32[2048,32]{0,1:T(8,128)}), f32[128,32]{0,1:T(8,128)}) %reduce-scatter.25.cloned.1.call-update) | async-done | bytes 16400 | tf_op jit(solution)/shard_map/reduce_scatter | solution.py:250
  1506.1 22.8 %all-reduce.29.cloned.1.call-done = f32[128,256]{1,0:T(8,128)} async-done(((f32[128,256]{1,0:T(8,128)}), f32[128,256]{1,0:T(8,128)}) %all-reduce.29.cloned.1.call-update) | async-done | bytes 131088 | tf_op jit(solution)/shard_map/psum | solution.py:256
  1528.8 183.2 %reduce-scatter.27.cloned.1.call-done = f32[2048,128]{1,0:T(8,128)} async-done(((f32[2048,2048]{1,0:T(8,128)}), f32[2048,128]{1,0:T(8,128)}) %reduce-scatter.27.cloned.1.call-update) | async-done | bytes 1048592 | tf_op jit(solution)/shard_map/reduce_scatter | solution.py:254
  1712.0 182.1 %reduce-scatter.19.cloned.1.call-done = f32[128,2048]{1,0:T(8,128)} async-done(((f32[2048,2048]{1,0:T(8,128)}), f32[128,2048]{1,0:T(8,128)}) %reduce-scatter.19.cloned.1.call-update) | async-done | bytes 1048592 | tf_op jit(solution)/shard_map/reduce_scatter | solution.py:247
  1894.1 182.1 %reduce-scatter.21.cloned.1.call-done = f32[128,2048]{1,0:T(8,128)} async-done(((f32[2048,2048]{1,0:T(8,128)}), f32[128,2048]{1,0:T(8,128)}) %reduce-scatter.21.cloned.1.call-update) | async-done | bytes 1048592 | tf_op jit(solution)/shard_map/reduce_scatter | solution.py:248
  (579 shorter events, 759.1 us)
Async XLA Ops:
  7.2 91.8 %copy-start.107 = (bf16[128,32]{0,1:T(8,128)(2,1)S(1)}, bf16[128,32]{0,1:T(8,128)(2,1)}, u32[]{:S(2)}) copy-start(bf16[128,32]{0,1:T(8,128)(2,1)} %param.30) | copy-start | bytes 24580
  7.2 110.9 %all-gather.14.cloned.1.call-start = ((), (), s32[]{:S(2)}) async-start(), calls=%async_computation.11 | async-start | bytes 1114112 | tf_op jit(solution)/shard_map/all_gather | solution.py:113
  8.0 110.2 %all-gather.10.cloned.1.call-start = ((), (), s32[]{:S(2)}) async-start(), calls=%async_computation.9 | async-start | bytes 6291456 | tf_op jit(solution)/shard_map/all_gather | solution.py:124
  37.3 161.7 %all-gather.12.cloned.1.call-start = ((), (), s32[]{:S(2)}) async-start(), calls=%async_computation.10 | async-start | bytes 8912896 | tf_op jit(solution)/shard_map/all_gather | solution.py:112
  38.1 457.8 %all-gather.16.cloned.1.call-start = ((), (), s32[]{:S(2)}) async-start(), calls=%async_computation.12 | async-start | bytes 8912896 | tf_op jit(solution)/shard_map/all_gather | solution.py:111
  38.6 479.8 %all-gather.20.cloned.1.call-start = ((), (), s32[]{:S(2)}) async-start(), calls=%async_computation.15 | async-start | bytes 6291456 | tf_op jit(solution)/shard_map/all_gather | solution.py:173
  39.2 479.2 %all-gather.18.cloned.1.call-start = ((), (), s32[]{:S(2)}) async-start(), calls=%async_computation.13 | async-start | bytes 8912896 | tf_op jit(solution)/shard_map/all_gather | solution.py:118
  39.8 1085.2 %reduce-scatter.17.cloned.1.call-start = ((), (), s32[]{:S(2)}) async-start(), calls=%async_computation.17 | async-start | bytes 1572864 | tf_op jit(solution)/shard_map/reduce_scatter | solution.py:215
  97.3 116.2 %copy-start.73 = (f32[2048]{0:T(1024)}, f32[2048]{0:T(1024)S(1)}, u32[]{:S(2)}) copy-start(f32[2048]{0:T(1024)S(1)} %mul.842) | copy-start | bytes 24580
  97.5 116.0 %copy-start.75 = (f32[2048]{0:T(1024)}, f32[2048]{0:T(1024)S(1)}, u32[]{:S(2)}) copy-start(f32[2048]{0:T(1024)S(1)} %mul.856) | copy-start | bytes 24580
  124.1 130.9 %copy-start.10 = (f32[1,1024,128]{2,1,0:T(8,128)}, f32[1,1024,128]{2,1,0:T(8,128)S(1)}, u32[]{:S(2)}) copy-start(f32[1,1024,128]{2,1,0:T(8,128)S(1)} %get-tuple-element.890) | copy-start | bytes 1572868
  124.1 159.1 %copy-start.14 = (f32[1,1024,128]{2,1,0:T(8,128)}, f32[1,1024,128]{2,1,0:T(8,128)S(1)}, u32[]{:S(2)}) copy-start(f32[1,1024,128]{2,1,0:T(8,128)S(1)} %get-tuple-element.891) | copy-start | bytes 1572868
  179.3 195.0 %copy-start.42 = (f32[4,256,32]{1,2,0:T(8,128)}, f32[4,256,32]{1,2,0:T(8,128)S(1)}, u32[]{:S(2)}) copy-start(f32[4,256,32]{1,2,0:T(8,128)S(1)} %copy.622) | copy-start | bytes 393220
  949.6 70.1 %copy-start.26 = (f32[1,1024,128]{2,1,0:T(8,128)S(1)}, f32[1,1024,128]{2,1,0:T(8,128)}, u32[]{:S(2)}) copy-start(f32[1,1024,128]{2,1,0:T(8,128)} %rev.39) | copy-start | bytes 1572868
  949.6 71.2 %copy-start.21 = (f32[1,1024,128]{2,1,0:T(8,128)S(1)}, f32[1,1024,128]{2,1,0:T(8,128)}, u32[]{:S(2)}) copy-start(f32[1,1024,128]{2,1,0:T(8,128)} %rev.40) | copy-start | bytes 1572868
  949.6 71.2 %copy-start.38 = (f32[4,256,128]{2,1,0:T(8,128)S(1)}, f32[4,256,128]{2,1,0:T(8,128)}, u32[]{:S(2)}) copy-start(f32[4,256,128]{2,1,0:T(8,128)} %fusion.134) | copy-start | bytes 1572868
  949.6 72.3 %copy-start.16 = (f32[1,1024,128]{2,1,0:T(8,128)S(1)}, f32[1,1024,128]{2,1,0:T(8,128)}, u32[]{:S(2)}) copy-start(f32[1,1024,128]{2,1,0:T(8,128)} %copy-done.14) | copy-start | bytes 1572868
  949.6 73.4 %copy-start.12 = (f32[1,1024,128]{2,1,0:T(8,128)S(1)}, f32[1,1024,128]{2,1,0:T(8,128)}, u32[]{:S(2)}) copy-start(f32[1,1024,128]{2,1,0:T(8,128)} %copy-done.10) | copy-start | bytes 1572868
  949.6 73.4 %copy-start.37 = (f32[4,256,128]{2,1,0:T(8,128)S(1)}, f32[4,256,128]{2,1,0:T(8,128)}, u32[]{:S(2)}) copy-start(f32[4,256,128]{2,1,0:T(8,128)} %fusion.137) | copy-start | bytes 1572868
  1095.3 127.0 %reduce-scatter.23.cloned.1.call-start = ((), (), s32[]{:S(2)}) async-start(), calls=%async_computation.20 | async-start | bytes 2228224 | tf_op jit(solution)/shard_map/reduce_scatter | solution.py:249
  1128.2 145.0 %reduce-scatter.29.cloned.1.call-start = ((), (), s32[]{:S(2)}) async-start(), calls=%async_computation.24 | async-start | bytes 139264
  1159.2 185.8 %reduce-scatter.15.cloned.1.call-start = ((), (), s32[]{:S(2)}) async-start(), calls=%async_computation.16 | async-start | bytes 12582912 | tf_op jit(solution)/shard_map/reduce_scatter | solution.py:214
  1201.7 245.0 %reduce-scatter.13.cloned.1.call-start = ((), (), s32[]{:S(2)}) async-start(), calls=%async_computation.14 | async-start | bytes 12582912 | tf_op jit(solution)/shard_map/reduce_scatter | solution.py:166
  1218.4 287.6 %reduce-scatter.25.cloned.1.call-start = ((), (), s32[]{:S(2)}) async-start(), calls=%async_computation.22 | async-start | bytes 278528 | tf_op jit(solution)/shard_map/reduce_scatter | solution.py:250
  1222.2 306.6 %all-reduce.29.cloned.1.call-start = ((), (), s32[]{:S(2)}) async-start(), calls=%async_computation.21 | async-start | bytes 262144 | tf_op jit(solution)/shard_map/psum | solution.py:256
  1223.0 489.0 %reduce-scatter.27.cloned.1.call-start = ((), (), s32[]{:S(2)}) async-start(), calls=%async_computation.23 | async-start | bytes 17825792 | tf_op jit(solution)/shard_map/reduce_scatter | solution.py:254
  1239.2 654.9 %reduce-scatter.19.cloned.1.call-start = ((), (), s32[]{:S(2)}) async-start(), calls=%async_computation.18 | async-start | bytes 17825792 | tf_op jit(solution)/shard_map/reduce_scatter | solution.py:247
  1254.8 821.5 %reduce-scatter.21.cloned.1.call-start = ((), (), s32[]{:S(2)}) async-start(), calls=%async_computation.19 | async-start | bytes 17825792 | tf_op jit(solution)/shard_map/reduce_scatter | solution.py:248
  1270.1 74.9 %copy-start.8 = (bf16[512,2048]{1,0:T(8,128)(2,1)S(1)}, bf16[512,2048]{1,0:T(8,128)(2,1)}, u32[]{:S(2)}) copy-start(bf16[512,2048]{1,0:T(8,128)(2,1)} %param.23) | copy-start | bytes 6291460
  1270.1 74.9 %copy-start.36 = (f32[512,256]{1,0:T(8,128)S(1)}, f32[512,256]{1,0:T(8,128)}, u32[]{:S(2)}) copy-start(f32[512,256]{1,0:T(8,128)} %reduce-scatter.17.cloned.1.call-done) | copy-start | bytes 1572868
  1270.1 74.9 %copy-start.72 = (f32[16,1,128]{2,1,0:T(1,128)S(1)}, f32[16,1,128]{2,1,0:T(1,128)}, u32[]{:S(2)}) copy-start(f32[16,1,128]{2,1,0:T(1,128)} %copy-done.71) | copy-start | bytes 24580
  1270.1 74.9 %copy-start.98 = (f32[512]{0:T(512)S(1)}, f32[512]{0:T(512)}, u32[]{:S(2)}) copy-start(f32[512]{0:T(512)} %copy-done.97) | copy-start | bytes 6148
  (112 other events, 1862.0 us)
Sparse Core Ops, SparseCore 0:
  10.2 40.6 all-gather.13
  52.4 55.6 all-gather.9
  110.3 74.9 all-gather.11
  187.3 73.1 all-gather.15
  261.9 54.9 all-gather.19
  319.0 78.0 all-gather.17
  1095.4 17.4 reduce-scatter.16
  1128.3 58.6 reduce-scatter.22
  1190.4 54.0 reduce-scatter.28
  1246.7 98.2 reduce-scatter.14
  1347.4 99.3 reduce-scatter.12
  1450.7 55.3 reduce-scatter.24
  1508.3 20.4 all-reduce.28
  1533.4 178.5 reduce-scatter.26
  1716.5 177.5 reduce-scatter.18
  1898.7 177.5 reduce-scatter.20
where the time goes:
time: 2100 us; the launch traced here: 2080 us
  waiting for transfers between devices  723 us (34%)
  matrix products  563 us (27%)
  local copies, waits for them, and re-layouts  303 us (14%)
  other arithmetic  302 us (14%)
  blocking collectives  174 us (8%)
    dot_general x6, matrix products, block_scan(): jnp.einsum('sctkh,sckhp->scthp', mixing, inputs, precision=HIGHEST)  257 us
    reduce_scatter x1, waiting for transfers between devices, on_device(): lax.psum_scatter(grad_out_weight, 'fsdp', scatter_dimension=1, tiled=True)  183 us
    reduce_scatter x1, waiting for transfers between devices, on_device(): lax.psum_scatter(grad_z_weight, 'fsdp', scatter_dimension=0, tiled=True)  182 us
    reduce_scatter x1, waiting for transfers between devices, on_device(): lax.psum_scatter(grad_x_weight, 'fsdp', scatter_dimension=0, tiled=True)  182 us
    reduce_scatter x1, waiting for transfers between devices, on_device(): lax.psum_scatter(partial_normed, 'tp', scatter_dimension=0, tiled=True)  71 us
    dot_general x6, matrix products, block_scan(): jnp.einsum('sckh,sckhp,sckn->schpn', to_last, inputs, b_mat, precision=HI...  70.2 us
    dot_general x6, matrix products, block_scan(): jnp.einsum('sctn,schpn->scthp', c_mat, entering, precision=HIGHEST)  65.3 us
    unnamed x1, blocking collectives  62.9 us
  transfers between devices with their start and end apart: 16, of which 7 were waited for; matrix products, arithmetic and copies ran while one was open for 28% of the time, Pallas kernels for 0%

commit v1 on v0

v1 whole, which is shorter than its diff:
```python
import functools

import jax
import jax.numpy as jnp
from jax import lax
from jax.experimental import pallas as pl
from jax.experimental.pallas import tpu as pltpu
from jax.sharding import PartitionSpec as P

P_SIZE = 64
N = 128
Q = 128
HG = 8
CG = HG * P_SIZE
MAX_PREFIX = 512
EPSILON = 1e-05
F32 = jnp.float32
BF16 = jnp.bfloat16
HIGHEST = lax.Precision.HIGHEST
NEG = -1e30
NN = ((1,), (0,))
NT = ((1,), (1,))
TN = ((0,), (0,))
MIB = 1024 * 1024


def dot(a, b, dims=NN):
    return lax.dot_general(a, b, (dims, ((), ())), preferred_element_type=F32)


def exact_dot(a, b, dims=NN):
    return lax.dot_general(
        a, b, (dims, ((), ())), precision=HIGHEST, preferred_element_type=F32
    )


def low(v):
    return v.astype(BF16)


def split_dot(v, e):
    hi = low(v)
    rest = low(v - hi.astype(F32))
    return dot(hi, e) + dot(rest, e)


def iota(shape, dim):
    return lax.broadcasted_iota(jnp.int32, shape, dim)


def sig(v):
    return 0.5 + 0.5 * jnp.tanh(0.5 * v)


def rows_of(c):
    return pl.ds(pl.multiple_of(c * Q, Q), Q)


def shifted_rows(x_ref, c):
    cur = x_ref[rows_of(c), :].astype(F32)
    start = pl.multiple_of(jnp.maximum(c * Q - 16, 0), 16)
    before = x_ref[pl.ds(start, 16), :].astype(F32)[8:]
    before = jnp.where(c > 0, before, 0.0)
    both = jnp.concatenate([before, cur], axis=0)
    return [cur] + [pltpu.roll(both, j, 0)[8:] for j in (1, 2, 3)]


def conv_of(shifted, taps):
    total = taps[3:4] * shifted[0]
    for j in (1, 2, 3):
        total = total + taps[3 - j : 4 - j] * shifted[j]
    return total


def spread_matrix(heads, width):
    return jnp.where(
        iota((heads, width), 1) // P_SIZE == iota((heads, width), 0), 1.0, 0.0
    ).astype(BF16)


def gather_matrix(width, lane0=0):
    return jnp.where(
        iota((width, 128), 0) // P_SIZE + lane0 == iota((width, 128), 1), 1.0, 0.0
    ).astype(BF16)


def prep_kernel(bc_ref, dt_ref, taps_ref, decay_ref, bias_ref, act_ref, cols_ref, rows_ref):
    heads = dt_ref.shape[1]
    groups = cols_ref.shape[0]
    length = dt_ref.shape[0]
    taps = taps_ref[...]
    tri = jnp.where(iota((Q, Q), 0) >= iota((Q, Q), 1), 1.0, 0.0).astype(F32)
    place = [
        jnp.where(iota((heads, 128), 1) == iota((heads, 128), 0) + k * heads, 1.0, 0.0).astype(F32)
        for k in range(3)
    ]

    def body(c, _):
        conv = conv_of(shifted_rows(bc_ref, c), taps)
        act_ref[rows_of(c), :] = low(conv * sig(conv))
        raw = dt_ref[rows_of(c), :] + bias_ref[...]
        step = jnp.maximum(raw, 0.0) + jnp.log(1.0 + jnp.exp(-jnp.abs(raw)))
        rate = -jnp.exp(decay_ref[...]) * step
        cum = exact_dot(tri, rate)
        packed = (
            exact_dot(cum, place[0])
            + exact_dot(cum - rate, place[1])
            + exact_dot(step, place[2])
        )
        turned = packed.T
        for g in range(groups):
            pick = jnp.where(
                (iota((128, 128), 0) == (iota((128, 128), 1) // HG) * heads + g * HG + iota((128, 128), 1) % HG)
                & (iota((128, 128), 1) < 3 * HG),
                1.0,
                0.0,
            ).astype(F32)
            cols_ref[g, rows_of(c), :] = exact_dot(packed, pick)
            rows_ref[g, 0:HG, rows_of(c)] = turned[g * HG : g * HG + HG]
            rows_ref[g, HG : 2 * HG, rows_of(c)] = turned[heads + g * HG : heads + g * HG + HG]
        return 0

    lax.fori_loop(0, length // Q, body, 0)


def prep(bc_pre, dt_pre, bc_taps, log_decay, dt_bias):
    length, heads = dt_pre.shape
    groups = heads // HG
    return pl.pallas_call(
        prep_kernel,
        out_shape=(
            jax.ShapeDtypeStruct((length, 2 * N), BF16),
            jax.ShapeDtypeStruct((groups, length, 128), F32),
            jax.ShapeDtypeStruct((groups, 2 * HG, length), F32),
        ),
        compiler_params=pltpu.CompilerParams(vmem_limit_bytes=32 * MIB),
        name="prep",
    )(bc_pre, dt_pre, bc_taps, log_decay[None], dt_bias[None])


def chunk_scalars(cols_ref, c, spread):
    part = cols_ref[0, rows_of(c), :]
    cum = part[:, 0:HG]
    ecum = part[:, HG : 2 * HG]
    step = part[:, 2 * HG : 3 * HG]
    last = cum[Q - 1 : Q, :]
    return cum, ecum, step, last


def prefix_column(prefix, c):
    return jnp.where(iota((Q, 1), 0) + c * Q < prefix, 1.0, 0.0).astype(F32)


def forward_kernel(
    prefix_ref, x_ref, taps_ref, skip_ref, cols_ref, rows_ref, act_ref, out_ref, xd_ref, kept_ref, back_ref, state_ref
):
    length, width = x_ref.shape
    chunks = length // Q
    anti = min(MAX_PREFIX // Q, chunks)
    prefix = prefix_ref[0]
    taps = taps_ref[...].astype(F32)
    skip = skip_ref[...]
    spread = spread_matrix(HG, width)
    lane_low = iota((1, 128), 1) < P_SIZE

    def stage_a(c, _):
        conv = conv_of(shifted_rows(x_ref, c), taps)
        x = conv * sig(conv)
        _, _, step, _ = chunk_scalars(cols_ref, c, spread)
        xd_ref[rows_of(c), :] = low(x * split_dot(step, spread))
        kept_ref[rows_of(c), :] = x * skip
        return 0

    lax.fori_loop(0, chunks, stage_a, 0)

    state_ref[...] = jnp.zeros_like(state_ref)
    back_ref[anti - 1] = jnp.zeros_like(back_ref[anti - 1])
    for c in range(anti - 1, 0, -1):
        cum, ecum, _, last = chunk_scalars(cols_ref, c, spread)
        weight = split_dot(jnp.exp(ecum) * prefix_column(prefix, c), spread)
        grow = split_dot(jnp.exp(cum[Q - 8 :]), spread)[7:8]
        b_mat = act_ref[rows_of(c), 0:N]
        xw = low(xd_ref[rows_of(c), :].astype(F32) * weight)
        state_ref[...] = state_ref[...] * grow + dot(b_mat, xw, TN)
        back_ref[c - 1] = low(state_ref[...])

    state_ref[...] = jnp.zeros_like(state_ref)
    causal_bias = jnp.where(iota((Q, Q), 1) <= iota((Q, Q), 0), 0.0, NEG).astype(F32)

    def chunk_body(c, two_way):
        b_mat = act_ref[rows_of(c), 0:N]
        c_mat = act_ref[rows_of(c), N : 2 * N]
        products = dot(c_mat, b_mat, NT)
        cum, ecum, _, last = chunk_scalars(cols_ref, c, spread)
        entering = split_dot(jnp.exp(cum), spread)
        total = kept_ref[rows_of(c), :] + dot(c_mat, low(state_ref[...])) * entering
        if two_way:
            leaving = split_dot(jnp.exp(last - ecum), spread)
            total = total + dot(c_mat, back_ref[c]) * leaving
            anti_bias = jnp.where(
                (iota((Q, Q), 1) > iota((Q, Q), 0)) & (iota((Q, Q), 1) + c * Q < prefix), 0.0, NEG
            ).astype(F32)
        xd = xd_ref[rows_of(c), :]
        rows = rows_ref[0, :, rows_of(c)]
        parts = []
        for pair in range(HG // 2):
            mixes = []
            for h in (2 * pair, 2 * pair + 1):
                e = cum[:, h : h + 1] - rows[h : h + 1] + causal_bias
                if two_way:
                    back = rows[HG + h : HG + h + 1] - ecum[:, h : h + 1] + anti_bias
                    e = jnp.maximum(e, back)
                mixes.append(low(jnp.exp(e) * products))
            x_pair = xd[:, pair * 128 : pair * 128 + 128]
            zero = jnp.zeros_like(x_pair)
            blocks = jnp.concatenate(
                [jnp.where(lane_low, x_pair, zero), jnp.where(lane_low, zero, x_pair)], axis=0
            )
            parts.append(dot(jnp.concatenate(mixes, axis=1), blocks))
        out_ref[rows_of(c), :] = (total + jnp.concatenate(parts, axis=1)).astype(out_ref.dtype)
        weight = split_dot(jnp.exp(last - cum), spread)
        xw = low(xd.astype(F32) * weight)
        state_ref[...] = state_ref[...] * entering[Q - 1 : Q] + dot(b_mat, xw, TN)
        return 0

    lax.fori_loop(0, anti, lambda c, _: chunk_body(c, True), 0)
    if chunks > anti:
        lax.fori_loop(anti, chunks, lambda c, _: chunk_body(c, False), 0)


def scan_forward(prefix, x_pre, taps, skip, cols, rows, act, out_type=BF16):
    length, channels = x_pre.shape
    groups = channels // CG
    anti = min(MAX_PREFIX // Q, length // Q)
    return pl.pallas_call(
        forward_kernel,
        grid=(groups,),
        in_specs=[
            pl.BlockSpec(memory_space=pltpu.SMEM),
            pl.BlockSpec((length, CG), lambda g: (0, g)),
            pl.BlockSpec((4, CG), lambda g: (0, g)),
            pl.BlockSpec((1, CG), lambda g: (0, g)),
            pl.BlockSpec((1, length, 128), lambda g: (g, 0, 0)),
            pl.BlockSpec((1, 2 * HG, length), lambda g: (g, 0, 0)),
            pl.BlockSpec((length, 2 * N), lambda g: (0, 0)),
        ],
        out_specs=pl.BlockSpec((length, CG), lambda g: (0, g)),
        out_shape=jax.ShapeDtypeStruct((length, channels), out_type),
        scratch_shapes=[
            pltpu.VMEM((length, CG), BF16),
            pltpu.VMEM((length, CG), F32),
            pltpu.VMEM((anti, N, CG), BF16),
            pltpu.VMEM((N, CG), F32),
        ],
        compiler_params=pltpu.CompilerParams(vmem_limit_bytes=40 * MIB),
        cost_estimate=pl.CostEstimate(
            flops=length * channels * 1024, bytes_accessed=length * channels * 6, transcendentals=length * channels * 4
        ),
        name="scan_forward",
    )(prefix, x_pre, taps, skip, cols, rows, act)


def backward_kernel(
    prefix_ref,
    x_ref,
    gate_ref,
    ssd_ref,
    gp_ref,
    norm_ref,
    taps_ref,
    skip_ref,
    gain_ref,
    cols_ref,
    rows_ref,
    act_ref,
    ggate_ref,
    gx_ref,
    gact_ref,
    gcols_ref,
    grows_ref,
    gsum_ref,
    x_scr,
    slope_scr,
    dy_scr,
    states_scr,
    dback_scr,
    state_ref,
    dstate_ref,
    next_scr,
):
    length, width = x_ref.shape
    chunks = length // Q
    anti = min(MAX_PREFIX // Q, chunks)
    prefix = prefix_ref[0]
    taps = taps_ref[...].astype(F32)
    skip = skip_ref[...]
    gain = gain_ref[...]
    spread = spread_matrix(HG, width)
    collect = gather_matrix(width)
    lane_low = iota((1, 128), 1) < P_SIZE

    gsum_ref[...] = jnp.zeros_like(gsum_ref)
    state_ref[...] = jnp.zeros_like(state_ref)

    @pl.when(pl.program_id(0) == 0)
    def _():
        gact_ref[...] = jnp.zeros_like(gact_ref)

    def stage_a(c, two_way):
        conv = conv_of(shifted_rows(x_ref, c), taps)
        s = sig(conv)
        x = conv * s
        x_scr[rows_of(c), :] = low(x)
        slope_scr[rows_of(c), :] = s + x * (1.0 - s)
        norm = norm_ref[rows_of(c), :]
        inv, coef = norm[:, 0:1], norm[:, 1:2]
        z = gate_ref[rows_of(c), :].astype(F32)
        y = ssd_ref[rows_of(c), :].astype(F32)
        gp = gp_ref[rows_of(c), :].astype(F32)
        sg = sig(z)
        act = z * sg
        gated = y * act
        gsum_ref[5:6, :] += jnp.sum(gp * gated * inv, axis=0, keepdims=True)
        gg = inv * gain * gp - gated * coef
        dy = gg * act
        ggate_ref[rows_of(c), :] = low(gg * y * (sg + act * (1.0 - sg)))
        dy_scr[rows_of(c), :] = low(dy)
        gsum_ref[4:5, :] += jnp.sum(dy * x, axis=0, keepdims=True)
        cum, ecum, step, last = chunk_scalars(cols_ref, c, spread)
        states_scr[c] = low(state_ref[...])
        entering = split_dot(jnp.exp(cum[Q - 8 :]), spread)
        weight = split_dot(jnp.exp(last - cum) * step, spread)
        b_mat = act_ref[rows_of(c), 0:N]
        c_mat = act_ref[rows_of(c), N : 2 * N]
        state_ref[...] = state_ref[...] * entering[7:8] + dot(b_mat, low(x * weight), TN)
        if two_way:
            leaving = split_dot(jnp.exp(last - ecum), spread)
            dback_scr[c + 1] = low(
                dback_scr[c].astype(F32) * entering[7:8] + dot(c_mat, low(dy * leaving), TN)
            )
        return 0

    dback_scr[0] = jnp.zeros_like(dback_scr[0])
    lax.fori_loop(0, anti, lambda c, _: stage_a(c, True), 0)
    if chunks > anti:
        lax.fori_loop(anti, chunks, lambda c, _: stage_a(c, False), 0)

    state_ref[...] = jnp.zeros_like(state_ref)
    dstate_ref[...] = jnp.zeros_like(dstate_ref)
    next_scr[...] = jnp.zeros_like(next_scr)
    s_idx, t_idx = iota((Q, Q), 0), iota((Q, Q), 1)
    causal_bias = jnp.where(s_idx <= t_idx, 0.0, NEG).astype(F32)
    from_r = jnp.where(s_idx >= t_idx, 1.0, 0.0)
    upto_r = jnp.where(s_idx <= t_idx, 1.0, 0.0)
    zero_q = jnp.zeros((Q, Q), F32)

    def twice(m):
        return low(
            jnp.concatenate(
                [jnp.concatenate([m, zero_q], axis=1), jnp.concatenate([zero_q, m], axis=1)], axis=0
            )
        )

    from_pair, upto_pair = twice(from_r), twice(upto_r)
    pair_s, pair_r = iota((Q, 2 * Q), 0), iota((Q, 2 * Q), 1) % Q
    before_pair = pair_s < pair_r
    after_pair = pair_s > pair_r
    sum_from = jnp.where(t_idx >= s_idx, 1.0, 0.0)
    sum_before = jnp.where(t_idx < s_idx, 1.0, 0.0)
    sum_upto = jnp.where(t_idx <= s_idx, 1.0, 0.0)
    sum_after = jnp.where(t_idx > s_idx, 1.0, 0.0)

    def chunk_body(c, two_way):
        b_mat = act_ref[rows_of(c), 0:N]
        c_mat = act_ref[rows_of(c), N : 2 * N]
        products = dot(b_mat, c_mat, NT)
        cum, ecum, step, last = chunk_scalars(cols_ref, c, spread)
        rows = rows_ref[0, :, rows_of(c)]
        x = x_scr[rows_of(c), :].astype(F32)
        dy_low = dy_scr[rows_of(c), :]
        dy = dy_low.astype(F32)
        step_wide = split_dot(step, spread)
        xd = x * step_wide
        xd_low = low(xd)
        if two_way:
            anti_bias = jnp.where((s_idx > t_idx) & (s_idx + c * Q < prefix), 0.0, NEG).astype(F32)
        dprod = jnp.zeros((Q, Q), F32)
        parts, inner = [], []
        for pair in range(HG // 2):
            lanes = slice(pair * 128, pair * 128 + 128)
            dy_pair = dy_low[:, lanes]
            zero = jnp.zeros_like(dy_pair)
            blocks = jnp.concatenate(
                [jnp.where(lane_low, dy_pair, zero), jnp.where(lane_low, zero, dy_pair)], axis=0
            )
            dmix = dot(xd_low[:, lanes], blocks, NT)
            mixes, moved = [], []
            for k in (0, 1):
                h = 2 * pair + k
                e = rows[h : h + 1] - cum[:, h : h + 1] + causal_bias
                if two_way:
                    back = ecum[:, h : h + 1] - rows[HG + h : HG + h + 1] + anti_bias
                    e = jnp.maximum(e, back)
                decay = jnp.exp(e)
                slab = dmix[:, k * Q : k * Q + Q] * decay
                dprod = dprod + slab
                mixes.append(low(decay * products))
                moved.append(low(slab * products))
            parts.append(dot(jnp.concatenate(mixes, axis=1), blocks))
            both = jnp.concatenate(moved, axis=1)
            crossing = jnp.where(before_pair, dot(both, from_pair), 0.0)
            if two_way:
                crossing = jnp.where(after_pair, dot(both, upto_pair), crossing)
            inner.append(jnp.sum(crossing, axis=0, keepdims=True))
        for pair in range(HG // 2):
            for k in (0, 1):
                h = 2 * pair + k
                grows_ref[0, h : h + 1, rows_of(c)] = inner[pair][:, k * Q : k * Q + Q]

        entering = split_dot(jnp.exp(cum), spread)
        to_last = split_dot(jnp.exp(last - cum), spread)
        grow = entering[Q - 1 : Q]
        dstate_low = low(dstate_ref[...])
        state_in = states_scr[c]
        du_carry = dot(b_mat, dstate_low) * to_last
        du = jnp.concatenate(parts, axis=1) + du_carry
        y_in = dot(c_mat, state_in) * entering
        dy_in = low(dy * entering)
        x_out = low(xd * to_last)
        d_c = dot(low(dprod), b_mat, TN) + dot(dy_in, state_in, NT)
        d_b = dot(low(dprod), c_mat) + dot(x_out, dstate_low, NT)
        qk = exact_dot(sum_from, dot(low(dy * y_in), collect)) + exact_dot(
            sum_before, dot(low(xd * du_carry), collect)
        )
        across = jnp.sum(dstate_ref[...] * state_in.astype(F32), axis=0, keepdims=True) * grow
        if two_way:
            back_state = state_ref[...]
            back_low = low(back_state)
            dback_low = dback_scr[c]
            leaving = split_dot(jnp.exp(last - ecum), spread)
            from_first = split_dot(jnp.exp(ecum) * prefix_column(prefix, c), spread)
            du_back = dot(b_mat, dback_low) * from_first
            du = du + du_back
            y_back = dot(c_mat, back_low) * leaving
            x_back = low(xd * from_first)
            d_c = d_c + dot(low(dy * leaving), back_low, NT)
            d_b = d_b + dot(x_back, dback_low, NT)
            qk = (
                qk
                + exact_dot(sum_upto, dot(low(dy * y_back), collect))
                + exact_dot(sum_after, dot(low(xd * du_back), collect))
            )
            across = across + grow * jnp.sum(
                dback_low.astype(F32) * back_state, axis=0, keepdims=True
            )
            state_ref[...] = back_state * grow + dot(b_mat, x_back, TN)
        dstate_ref[...] = dstate_ref[...] * grow + dot(c_mat, dy_in, TN)
        gact_ref[rows_of(c), 0:N] += d_b
        gact_ref[rows_of(c), N : 2 * N] += d_c
        direct = dot(low(x * du), collect)
        across8 = split_dot(jnp.broadcast_to(across, (8, width)), collect)
        gcols_ref[0, rows_of(c), 0:128] = direct
        gcols_ref[0, rows_of(c), 128:256] = qk + across8[0:1]

        dconv = (du * step_wide + skip * dy) * slope_scr[rows_of(c), :]
        shifted = shifted_rows(x_ref, c)
        both = jnp.concatenate([dconv, next_scr[...]], axis=0)
        gx = taps[3:4] * dconv
        gsum_ref[3:4, :] += jnp.sum(dconv * shifted[0], axis=0, keepdims=True)
        for j in (1, 2, 3):
            gx = gx + taps[3 - j : 4 - j] * pltpu.roll(both, Q + 8 - j, 0)[:Q]
            gsum_ref[3 - j : 4 - j, :] += jnp.sum(dconv * shifted[j], axis=0, keepdims=True)
        gx_ref[rows_of(c), :] = low(gx)
        next_scr[...] = dconv[0:8]
        return 0

    if chunks > anti:
        lax.fori_loop(0, chunks - anti, lambda i, _: chunk_body(chunks - 1 - i, False), 0)
    lax.fori_loop(0, anti, lambda i, _: chunk_body(anti - 1 - i, True), 0)


def scan_backward(prefix, x_pre, gate_pre, ssd_out, grad_projected, norm, taps, skip, gain, cols, rows, act):
    length, channels = x_pre.shape
    groups = channels // CG
    chunks = length // Q
    anti = min(MAX_PREFIX // Q, chunks)
    wide = pl.BlockSpec((length, CG), lambda g: (0, g))
    return pl.pallas_call(
        backward_kernel,
        grid=(groups,),
        in_specs=[
            pl.BlockSpec(memory_space=pltpu.SMEM),
            wide,
            wide,
            wide,
            wide,
            pl.BlockSpec((length, 2), lambda g: (0, 0)),
            pl.BlockSpec((4, CG), lambda g: (0, g)),
            pl.BlockSpec((1, CG), lambda g: (0, g)),
            pl.BlockSpec((1, CG), lambda g: (0, g)),
            pl.BlockSpec((1, length, 128), lambda g: (g, 0, 0)),
            pl.BlockSpec((1, 2 * HG, length), lambda g: (g, 0, 0)),
            pl.BlockSpec((length, 2 * N), lambda g: (0, 0)),
        ],
        out_specs=[
            wide,
            wide,
            pl.BlockSpec((length, 2 * N), lambda g: (0, 0)),
            pl.BlockSpec((1, length, 256), lambda g: (g, 0, 0)),
            pl.BlockSpec((1, HG, length), lambda g: (g, 0, 0)),
            pl.BlockSpec((8, CG), lambda g: (0, g)),
        ],
        out_shape=(
            jax.ShapeDtypeStruct((length, channels), BF16),
            jax.ShapeDtypeStruct((length, channels), BF16),
            jax.ShapeDtypeStruct((length, 2 * N), F32),
            jax.ShapeDtypeStruct((groups, length, 256), F32),
            jax.ShapeDtypeStruct((groups, HG, length), F32),
            jax.ShapeDtypeStruct((8, channels), F32),
        ),
        scratch_shapes=[
            pltpu.VMEM((length, CG), BF16),
            pltpu.VMEM((length, CG), F32),
            pltpu.VMEM((length, CG), BF16),
            pltpu.VMEM((chunks, N, CG), BF16),
            pltpu.VMEM((anti + 1, N, CG), BF16),
            pltpu.VMEM((N, CG), F32),
            pltpu.VMEM((N, CG), F32),
            pltpu.VMEM((8, CG), F32),
        ],
        compiler_params=pltpu.CompilerParams(vmem_limit_bytes=48 * MIB),
        cost_estimate=pl.CostEstimate(
            flops=length * channels * 4096, bytes_accessed=length * channels * 14, transcendentals=length * channels * 8
        ),
        name="scan_backward",
    )(prefix, x_pre, gate_pre, ssd_out, grad_projected, norm, taps, skip, gain, cols, rows, act)


def post_kernel(
    bc_ref, dt_ref, taps_ref, decay_ref, bias_ref, gact_ref, gcols_ref, grows_ref, gbc_ref, gdt_ref, gtaps_ref, ghead_ref, next_scr
):
    length, heads = dt_ref.shape
    groups = gcols_ref.shape[0]
    chunks = length // Q
    taps = taps_ref[...]
    gtaps_ref[...] = jnp.zeros_like(gtaps_ref)
    ghead_ref[...] = jnp.zeros_like(ghead_ref)
    next_scr[...] = jnp.zeros_like(next_scr)
    growth = -jnp.exp(decay_ref[...])
    bias = bias_ref[...]

    def body(i, _):
        c = chunks - 1 - i
        shifted = shifted_rows(bc_ref, c)
        conv = conv_of(shifted, taps)
        s = sig(conv)
        dconv = gact_ref[rows_of(c), :] * (s + conv * s * (1.0 - s))
        both = jnp.concatenate([dconv, next_scr[...]], axis=0)
        g = taps[3:4] * dconv
        gtaps_ref[3:4, :] += jnp.sum(dconv * shifted[0], axis=0, keepdims=True)
        for j in (1, 2, 3):
            g = g + taps[3 - j : 4 - j] * pltpu.roll(both, Q + 8 - j, 0)[:Q]
            gtaps_ref[3 - j : 4 - j, :] += jnp.sum(dconv * shifted[j], axis=0, keepdims=True)
        gbc_ref[rows_of(c), :] = g
        next_scr[...] = dconv[0:8]

        direct = jnp.zeros((Q, heads), F32)
        moved = jnp.zeros((Q, heads), F32)
        for g in range(groups):
            lift = jnp.where(
                (iota((128, heads), 1) == iota((128, heads), 0) + g * HG) & (iota((128, heads), 0) < HG), 1.0, 0.0
            ).astype(F32)
            direct = direct + exact_dot(gcols_ref[g, rows_of(c), 0:128], lift)
            moved = moved + exact_dot(gcols_ref[g, rows_of(c), 128:256], lift)
            moved = moved + exact_dot(grows_ref[g, :, rows_of(c)], lift[0:HG], TN)
        raw = dt_ref[rows_of(c), :] + bias
        step = jnp.maximum(raw, 0.0) + jnp.log(1.0 + jnp.exp(-jnp.abs(raw)))
        gdt = (direct + moved * growth) * sig(raw)
        gdt_ref[rows_of(c), :] = low(gdt)
        ghead_ref[0:1, :] += jnp.sum(moved * growth * step, axis=0, keepdims=True)
        ghead_ref[1:2, :] += jnp.sum(gdt, axis=0, keepdims=True)
        return 0

    lax.fori_loop(0, chunks, body, 0)


def post(bc_pre, dt_pre, bc_taps, log_decay, dt_bias, grad_act, gcols, grows):
    length, heads = dt_pre.shape
    return pl.pallas_call(
        post_kernel,
        out_shape=(
            jax.ShapeDtypeStruct((length, 2 * N), F32),
            jax.ShapeDtypeStruct((length, heads), BF16),
            jax.ShapeDtypeStruct((8, 2 * N), F32),
            jax.ShapeDtypeStruct((8, heads), F32),
        ),
        scratch_shapes=[pltpu.VMEM((8, 2 * N), F32)],
        compiler_params=pltpu.CompilerParams(vmem_limit_bytes=40 * MIB),
        name="post",
    )(bc_pre, dt_pre, bc_taps, log_decay[None], dt_bias[None], grad_act, gcols, grows)


def on_device(
    hidden,
    cotangent,
    prefix,
    input_norm_gain,
    z_weight,
    x_weight,
    bc_weight,
    dt_weight,
    x_conv,
    bc_conv,
    log_decay,
    dt_bias,
    skip_gain,
    gate_gain,
    out_weight,
):
    fsdp = lax.axis_size("fsdp")
    tp = lax.axis_size("tp")
    own, width = hidden.shape
    heads = log_decay.shape[0]
    channels = heads * P_SIZE
    all_channels = channels * tp
    length = own * tp
    taps_own = x_conv.shape[2]

    def gather(v):
        return lax.all_gather(v, "fsdp", axis=0, tiled=True)

    small = jnp.concatenate(
        [input_norm_gain.reshape(-1), x_conv.reshape(-1), bc_conv.reshape(-1), gate_gain.reshape(-1)]
    )
    sizes = [input_norm_gain.size, x_conv.size, bc_conv.size, gate_gain.size]
    rows = width // fsdp
    small_columns = -(-small.size // rows)
    tail = jnp.pad(small, (0, small_columns * rows - small.size)).reshape(rows, small_columns)
    first = jnp.concatenate([bc_weight, dt_weight, tail], axis=1)
    hidden_all = lax.all_gather(hidden, "tp", axis=0, tiled=True)
    first_all = gather(first)
    x_all = gather(x_weight)
    z_all = gather(z_weight)
    cot_all = lax.all_gather(cotangent, "tp", axis=0, tiled=True)
    out_all = gather(out_weight.T)

    bc_all = first_all[:, : 2 * N]
    dt_all = first_all[:, 2 * N : 2 * N + heads]
    small_all = first_all[:, 2 * N + heads :].reshape(fsdp, -1)
    cuts = [0]
    for size in sizes:
        cuts.append(cuts[-1] + size)
    norm_gain = small_all[:, cuts[0] : cuts[1]].reshape(-1).astype(F32)
    x_taps = small_all[:, cuts[1] : cuts[2]].reshape(fsdp, heads, 4, taps_own)
    x_taps = jnp.transpose(x_taps, (2, 1, 0, 3)).reshape(4, channels).astype(F32)
    bc_taps = small_all[:, cuts[2] : cuts[3]].reshape(fsdp, 4, -1)
    bc_taps = jnp.transpose(bc_taps, (1, 0, 2)).reshape(4, 2 * N).astype(F32)
    gain = small_all[:, cuts[3] : cuts[4]].reshape(fsdp, heads, -1)
    gain = jnp.transpose(gain, (1, 0, 2)).reshape(1, channels).astype(F32)
    skip = jnp.repeat(skip_gain, P_SIZE)[None]

    wide_all = hidden_all.astype(F32)
    inv_rms_all = lax.rsqrt(jnp.mean(wide_all * wide_all, axis=-1, keepdims=True) + EPSILON)
    normed = low(wide_all * inv_rms_all * norm_gain)
    bc_pre = dot(normed, bc_all)
    dt_pre = dot(normed, dt_all)
    x_pre = low(dot(normed, x_all))
    act, cols, head_rows = prep(bc_pre, dt_pre, bc_taps, log_decay, dt_bias)
    ssd_out = scan_forward(prefix, x_pre, x_taps, skip, cols, head_rows, act)

    gate_pre = dot(normed, z_all)
    gated = ssd_out.astype(F32) * (gate_pre * sig(gate_pre))
    square_sum = lax.psum(jnp.sum(gated * gated, axis=-1), "tp")
    gate_low = low(gate_pre)
    inv_gate = lax.rsqrt(square_sum / all_channels + EPSILON)[:, None]
    projected = low(gated * inv_gate * gain)

    grad_projected = dot(cot_all, out_all)
    dot_sum = lax.psum(jnp.sum(grad_projected * gain * gated, axis=-1), "tp")
    coef = inv_gate * inv_gate * inv_gate * (dot_sum / all_channels)[:, None]
    norm = jnp.concatenate([inv_gate, coef], axis=1)
    grad_low = low(grad_projected)

    def scatter_tp(v):
        return lax.psum_scatter(low(v), "tp", scatter_dimension=0, tiled=True).astype(F32)

    def scatter(v):
        return lax.psum_scatter(low(v), "fsdp", scatter_dimension=0, tiled=True).astype(F32)

    wide = hidden.astype(F32)
    branch = scatter_tp(dot(projected, out_all, NT))
    mixed = wide + branch
    grad_out = scatter(dot(cot_all, projected, TN))

    ggate, gx, gact, gcols, grows, gsum = scan_backward(
        prefix, x_pre, gate_low, ssd_out, grad_low, norm, x_taps, skip, gain, cols, head_rows, act
    )
    gbc_part, gdt, gbc_taps, ghead = post(
        bc_pre, dt_pre, bc_taps, log_decay, dt_bias, gact, gcols, grows
    )
    grad_z = scatter(dot(normed, ggate, TN))
    grad_x = scatter(dot(normed, gx, TN))
    gbc = low(lax.psum_scatter(gbc_part, "tp", scatter_dimension=0, tiled=True))
    part = dot(ggate, z_all, NT) + dot(gx, x_all, NT) + dot(gdt, dt_all, NT)
    grad_normed = scatter_tp(part) + dot(gbc, bc_all, NT)
    inv_rms = lax.rsqrt(jnp.mean(wide * wide, axis=-1, keepdims=True) + EPSILON)
    normed_own = low(wide * inv_rms * norm_gain)
    grad_rest = scatter(
        jnp.concatenate([dot(normed_own, gbc, TN), dot(normed, gdt, TN)], axis=1)
    )
    grad_gain = jnp.sum(grad_normed * wide * inv_rms, axis=0)
    scaled = grad_normed * norm_gain
    grad_hidden = (
        inv_rms * scaled
        - wide * inv_rms * inv_rms * inv_rms * jnp.mean(scaled * wide, axis=-1, keepdims=True)
        + cotangent.astype(F32)
    )
    gx_taps = jnp.transpose(gsum[0:4].reshape(4, heads, fsdp, taps_own), (2, 1, 0, 3))
    g_taps = jnp.transpose(gbc_taps[0:4].reshape(4, fsdp, -1), (1, 0, 2))
    g_gain = jnp.transpose(gsum[5].reshape(heads, fsdp, -1), (1, 0, 2))
    g_skip = jnp.sum(gsum[4].reshape(heads, P_SIZE), axis=-1)
    slices = jnp.concatenate(
        [
            grad_gain.reshape(fsdp, -1),
            g_taps.reshape(fsdp, -1),
            gx_taps.reshape(fsdp, -1),
            g_gain.reshape(fsdp, -1),
        ],
        axis=1,
    )
    mine = lax.psum_scatter(slices, "fsdp", scatter_dimension=0, tiled=True)[0]
    per_head = lax.psum(jnp.concatenate([ghead[0], ghead[1], g_skip]), "fsdp")
    n_norm, n_taps = input_norm_gain.size, bc_conv.size
    shared = n_norm + n_taps
    together = lax.psum(
        jnp.concatenate([grad_rest[:, : 2 * N].reshape(-1), mine[:shared]]), "tp"
    )
    bc_size = rows * 2 * N
    return (
        mixed,
        grad_hidden,
        together[bc_size : bc_size + n_norm],
        grad_z,
        grad_x,
        together[:bc_size].reshape(rows, 2 * N),
        grad_rest[:, 2 * N :],
        mine[shared : shared + x_conv.size].reshape(x_conv.shape),
        together[bc_size + n_norm :].reshape(bc_conv.shape),
        per_head[:heads],
        per_head[heads : 2 * heads],
        per_head[2 * heads :],
        mine[shared + x_conv.size :].reshape(gate_gain.shape),
        grad_out.T,
    )


def solution(mesh):
    both = P(("fsdp", "tp"), None)
    split = P("fsdp", "tp")
    ins = (
        both, both, P("fsdp"), P("fsdp"), split, split, P("fsdp", None), split, P("tp", None, "fsdp"),
        P(None, "fsdp"), P("tp"), P("tp"), P("tp"), P("tp", "fsdp"), P("tp", "fsdp"),
    )
    outs = (
        both, both, P("fsdp"), split, split, P("fsdp", None), split, P("tp", None, "fsdp"),
        P(None, "fsdp"), P("tp"), P("tp"), P("tp"), P("tp", "fsdp"), P("tp", "fsdp"),
    )
    return jax.shard_map(on_device, mesh=mesh, in_specs=ins, out_specs=outs, check_vma=False)
```

time: 2100 us -> 1120 us (0.53)
  matrix products: 563 us -> 157 us
  other arithmetic: 302 us -> 20 us
  local copies, waits for them, and re-layouts: 303 us -> 49.2 us
  Pallas kernels: 0 us -> 163 us
  blocking collectives: 174 us -> 71 us
  waiting for transfers between devices: 723 us -> 636 us
    reduce_scatter x8 -> x5, waiting for transfers between devices: 697 us -> 269 us  [the longest x2 212 us: scatter(): lax.psum_scatter(low(v), 'fsdp', scatter_dimension=0, tiled=True)]
    dot_general x39 -> x15, matrix products: 563 us -> 157 us  [dot(): return lax.dot_general(a, b, (dims, ((), ())), preferred_element_type=F32)]
    all_gather x5, waiting for transfers between devices: 0.02 us -> 247 us  [the longest x4 195 us: gather(): return lax.all_gather(v, 'fsdp', axis=0, tiled=True)]
    pallas_call x0 -> x4, Pallas kernels: none -> 163 us  [the longest x1 105 us: scan_backward(): pl.pallas_call(backward_kernel, grid=(groups,), in_specs=[pl.BlockSpec(me...]
    reduce_sum x19 -> x3, other arithmetic: 106 us -> 3.82 us  [the longest x1 3.22 us: on_device(): jnp.mean(wide_all * wide_all, axis=-1, keepdims=True) + EPSILON]
    all_gather x5 -> x0, blocking collectives: 96.2 us -> none  [the longest x1 23.2 us: on_device(): lax.all_gather(input_norm_gain, 'fsdp', axis=0, tiled=True)]
    reshape x25 -> x12, local copies, waits for them, and re-layouts: 95.3 us -> 4.81 us  [the longest x1 1.09 us: on_device(): gsum[0:4].reshape(4, heads, fsdp, taps_own)]
    unnamed x17 -> x16, waiting for transfers between devices: 3.8 us -> 77.6 us
  transfers between devices with their start and end apart: 16 -> 14, of which waited for: 7 -> 12; matrix products, arithmetic and copies ran while one was open for 28% -> 16% of each run, Pallas kernels for 0% -> 5%
where the time goes in v1:
time: 1120 us; the launch traced here: 1110 us
  waiting for transfers between devices  636 us (57%)
  Pallas kernels  163 us (15%)
  matrix products  157 us (14%)
  blocking collectives  71 us (6%)
  local copies, waits for them, and re-layouts  49.2 us (4%)
  other arithmetic  20 us (2%)
  between operations  15.5 us (1%)
    reduce_scatter x2, waiting for transfers between devices, scatter(): lax.psum_scatter(low(v), 'fsdp', scatter_dimension=0, tiled=True)  212 us
    all_gather x4, waiting for transfers between devices, gather(): return lax.all_gather(v, 'fsdp', axis=0, tiled=True)  195 us
    dot_general x15, matrix products, dot(): return lax.dot_general(a, b, (dims, ((), ())), preferred_element_type=F32)  157 us
    pallas_call x1, Pallas kernels, scan_backward(): pl.pallas_call(backward_kernel, grid=(groups,), in_specs=[pl.BlockSpec(me...  105 us
    unnamed x16, waiting for transfers between devices  77.6 us
    unnamed x1, blocking collectives  66 us
    reduce_scatter x2, waiting for transfers between devices, scatter_tp(): lax.psum_scatter(low(v), 'tp', scatter_dimension=0, tiled=True).astype(F32)  55.1 us
    all_gather x1, waiting for transfers between devices, on_device(): hidden_all = lax.all_gather(hidden, 'tp', axis=0, tiled=True)  52.8 us
  transfers between devices with their start and end apart: 14, of which 12 were waited for; matrix products, arithmetic and copies ran while one was open for 16% of the time, Pallas kernels for 5%

profile of v1, /device:TPU:0, one launch (start us, length us, event | category | flops | bytes accessed | tf_op | source)
XLA Modules:
  0.0 1113.3 jit_solution(7021360948698075967)
XLA Ops:
  17.9 37.9 %all-gather.9.cloned.1.call-done = bf16[2048,295]{1,0:T(8,128)(2,1)} async-done(((bf16[128,295]{1,0:T(8,128)(2,1)}), bf16[2048,295]{1,0:T(8,128)(2,1)}) %all-gather.9.cloned.1.call-update) | async-done | bytes 1208336 | tf_op jit(solution)/shard_map/all_gather | solution.py:630
  60.3 52.8 %all-gather.7.cloned.1.call-done = bf16[1024,2048]{1,0:T(8,128)(2,1)} async-done(((bf16[512,2048]{1,0:T(8,128)(2,1)}), bf16[1024,2048]{1,0:T(8,128)(2,1)}) %all-gather.7.cloned.1.call-update) | async-done | bytes 4194320 | tf_op jit(solution)/shard_map/all_gather | solution.py:640
  113.1 3.2 fusion
  120.5 9.7 prep.1
  131.6 58.6 %all-gather.11.cloned.1.call-done = bf16[2048,2048]{1,0:T(8,128)(2,1)} async-done(((bf16[128,2048]{1,0:T(8,128)(2,1)}), bf16[2048,2048]{1,0:T(8,128)(2,1)}) %all-gather.11.cloned.1.call-update) | async-done | bytes 8388624 | tf_op jit(solution)/shard_map/all_gather | solution.py:630
  190.2 12.6 %convolution_convert_fusion.3.x_ref = bf16[1024,2048]{1,0:T(8,128)(2,1)S(1)} fusion(bf16[1024,2048]{1,0:T(8,128)(2,1)} %copy-done.8, bf16[2048,2048]{1,0:T(8,128)(2,1)} %all-gather.11.cloned.1.call-done), kind=kOutput, calls=%fused_computation.31 | convolution fusion | flops 8592031744 | bytes 16777216 | tf_op jit(solution)/shard_map/dot_general | solution.py:28
  202.8 40.6 %scan_forward.1.ssd_ref = bf16[1024,2048]{1,0:T(8,128)(2,1)S(1)} custom-call(s32[1]{0:T(128)S(6)} %copy.127.prefix_ref, bf16[1024,2048]{1,0:T(8,128)(2,1)S(1)} %convolution_convert_fusion.3.x_ref, f32[4,2048]{1,0:T(4,128)S(1)} %reshape.173.taps_ref, f32[1,2048]{1,0:T(1,128)S(1)} %broadcast_in_dim_reshape.3.skip_ref, f32[4,1024,128]{2,1,0:T(8,128)S(1)} %copy-done.4, ...), custom_call_target="tpu_custom_call" | custom-call | flops 2147483648 | bytes 12582912 | tf_op jit(solution)/shard_map/scan_forward/pallas_call | solution.py:235
  247.4 18.0 %all-gather.13.cloned.1.call-done = bf16[2048,2048]{1,0:T(8,128)(2,1)} async-done(((bf16[128,2048]{1,0:T(8,128)(2,1)}), bf16[2048,2048]{1,0:T(8,128)(2,1)}) %all-gather.13.cloned.1.call-update) | async-done | bytes 8388624 | tf_op jit(solution)/shard_map/all_gather | solution.py:630
  265.4 14.6 %fusion.35 = f32[1024,2048]{1,0:T(8,128)} fusion(bf16[1024,2048]{1,0:T(8,128)(2,1)} %copy-done.8, bf16[2048,2048]{1,0:T(8,128)(2,1)} %all-gather.13.cloned.1.call-done), kind=kOutput, calls=%fused_computation.78 | convolution fusion | flops 8589934592 | bytes 20971520 | tf_op jit(solution)/shard_map/dot_general | solution.py:28
  280.0 41.9 %all-gather.17.cloned.1.call-done = bf16[1024,2048]{1,0:T(8,128)(2,1)} async-done(((bf16[512,2048]{1,0:T(8,128)(2,1)}), bf16[1024,2048]{1,0:T(8,128)(2,1)}) %all-gather.17.cloned.1.call-update) | async-done | bytes 4194320 | tf_op jit(solution)/shard_map/all_gather | solution.py:644
  321.9 80.1 %all-gather.15.cloned.1.call-done = bf16[2048,2048]{0,1:T(8,128)(2,1)} async-done(((bf16[128,2048]{0,1:T(8,128)(2,1)}), bf16[2048,2048]{0,1:T(8,128)(2,1)}) %all-gather.15.cloned.1.call-update) | async-done | bytes 8388624 | tf_op jit(solution)/shard_map/all_gather | solution.py:630
  402.0 20.7 %multiply_reduce_fusion = (f32[1024]{0:T(1024)S(1)}, f32[1024]{0:T(1024)S(1)}, bf16[1024,2048]{1,0:T(8,128)(2,1)}, bf16[1024,2048]{1,0:T(8,128)(2,1)}) fusion(f32[2048]{0:T(1024)S(1)} %reshape.175, f32[1024,2048]{1,0:T(8,128)} %fusion.35, bf16[1024,2048]{1,0:T(8,128)(2,1)} %copy-done.6, bf16[1024,2048]{1,0:T(8,128)(2,1)} %all-gather.17.cloned.1.call-done, ...), kind=kOutput, calls=%fused_computation.7 | convolution fusion | flops 8617195520 | bytes 33570816 | tf_op jit(solution)/shard_map/dot_general | solution.py:28
  422.7 5.0 all-reduce.3
  429.6 104.9 %scan_backward.1 = (bf16[1024,2048]{1,0:T(8,128)(2,1)}, bf16[1024,2048]{1,0:T(8,128)(2,1)}, f32[1024,256]{1,0:T(8,128)S(1)}, f32[4,1024,256]{2,1,0:T(8,128)}, f3...) custom-call(s32[1]{0:T(128)S(6)} %copy.127.prefix_ref, bf16[1024,2048]{1,0:T(8,128)(2,1)} %copy-done.7, ...), custom_call_target="tpu_custom_call" | custom-call | flops 8589934592 | bytes 29360128 | tf_op jit(solution)/shard_map/scan_backward/pallas_call | solution.py:488
  536.7 8.2 post.1
  545.2 3.2 convolution_convert_fusion.5
  548.6 13.6 %fusion.36 = f32[1024,2048]{1,0:T(8,128)} fusion(bf16[1024,2048]{1,0:T(8,128)(2,1)S(1)} %copy-done.16, bf16[2048,2048]{1,0:T(8,128)(2,1)} %all-gather.13.cloned.1.call-done), kind=kOutput, calls=%fused_computation.79 | convolution fusion | flops 8589934592 | bytes 20971520 | tf_op jit(solution)/shard_map/dot_general | solution.py:28
  567.9 12.6 %fusion.37 = f32[1024,2048]{1,0:T(8,128)S(1)} fusion(bf16[1024,2048]{1,0:T(8,128)(2,1)} %get-tuple-element.31, bf16[2048,2048]{1,0:T(8,128)(2,1)} %all-gather.11.cloned.1.call-done), kind=kOutput, calls=%fused_computation.80 | convolution fusion | flops 8589934592 | bytes 20971520 | tf_op jit(solution)/shard_map/dot_general | solution.py:28
  580.4 7.0 add_convert_fusion
  587.8 16.5 %convolution_convert_fusion.2 = bf16[1024,2048]{1,0:T(8,128)(2,1)} fusion(bf16[2048,2048]{0,1:T(8,128)(2,1)} %all-gather.15.cloned.1.call-done, f32[2048]{0:T(1024)S(1)} %reshape.175, f32[1024]{0:T(1024)S(1)} %get-tuple-element.129, f32[1024,2048]{1,0:T(8,128)} %fusion.35, bf16[1024,2048]{1,0:T(8,128)(2,1)} %copy-done.6), kind=kOutput, calls=%fused_computation.30 | convolution fusion | flops 8610906112 | bytes 25178112 | tf_op jit(solution)/shard_map/dot_general | solution.py:28
  608.5 19.0 %reduce-scatter.23.cloned.1.call-done = bf16[128,288]{1,0:T(8,128)(2,1)} async-done(((bf16[2048,288]{1,0:T(8,128)(2,1)}), bf16[128,288]{1,0:T(8,128)(2,1)}) %reduce-scatter.23.cloned.1.call-update) | async-done | bytes 73744
  628.6 55.1 %reduce-scatter.15.cloned.1.call-done = bf16[512,2048]{1,0:T(8,128)(2,1)} async-done(((bf16[1024,2048]{1,0:T(8,128)(2,1)}), bf16[512,2048]{1,0:T(8,128)(2,1)}) %reduce-scatter.15.cloned.1.call-update) | async-done | bytes 2097168 | tf_op jit(solution)/shard_map/reduce_scatter | solution.py:685
  683.7 5.6 fusion.13
  689.5 66.0 %all-reduce.2 = (f32[16,832]{0,1:T(8,128)S(1)}, f32[96]{0:T(128)S(1)}) all-reduce(f32[16,832]{0,1:T(8,128)S(1)} %pad_maximum_fusion.1, f32[96]{0:T(128)S(1)} %pad_maximum_fusion.5), channel_id=6, replica_groups=mesh['fsdp'=16,'tp'=2] {'fsdp'}, use_global_device_ids=true, to_apply=%region_12.13.clone | all-reduce | flops 13408 | bytes 107264
  757.3 16.6 %convert_bitcast_fusion = bf16[2048,2048]{0,1:T(8,128)(2,1)} fusion(bf16[1024,2048]{1,0:T(8,128)(2,1)} %all-gather.17.cloned.1.call-done, f32[2048]{0:T(1024)S(1)} %reshape.175, f32[1024]{0:T(1024)S(1)} %get-tuple-element.129, f32[1024,2048]{1,0:T(8,128)} %fusion.35, bf16[1024,2048]{1,0:T(8,128)(2,1)} %copy-done.6), kind=kOutput, calls=%fused_computation.5 | convolution fusion | flops 8613003264 | bytes 25178112 | tf_op jit(solution)/shard_map/dot_general | solution.py:28
  773.9 12.4 %copy.121 = bf16[2048,2048]{1,0:T(8,128)(2,1)} copy(bf16[2048,2048]{0,1:T(8,128)(2,1)} %convert_bitcast_fusion) | data formatting | bytes 16777216
  786.4 14.4 %convolution_convert_fusion.1 = bf16[2048,2048]{1,0:T(8,128)(2,1)} fusion(bf16[1024,2048]{1,0:T(8,128)(2,1)} %copy-done.8, bf16[1024,2048]{1,0:T(8,128)(2,1)} %get-tuple-element.30), kind=kOutput, calls=%fused_computation.17 | convolution fusion | flops 8594128896 | bytes 16777216 | tf_op jit(solution)/shard_map/dot_general | solution.py:28
  801.1 14.6 %convolution_convert_fusion = bf16[2048,2048]{1,0:T(8,128)(2,1)} fusion(bf16[1024,2048]{1,0:T(8,128)(2,1)} %copy-done.8, bf16[1024,2048]{1,0:T(8,128)(2,1)} %get-tuple-element.31), kind=kOutput, calls=%fused_computation.16 | convolution fusion | flops 8594128896 | bytes 16777216 | tf_op jit(solution)/shard_map/dot_general | solution.py:28
  821.2 6.6 fusion.8
  832.0 55.4 %reduce-scatter.25.cloned.1.call-done = bf16[128,2048]{1,0:T(8,128)(2,1)} async-done(((bf16[2048,2048]{1,0:T(8,128)(2,1)}), bf16[128,2048]{1,0:T(8,128)(2,1)}) %reduce-scatter.25.cloned.1.call-update) | async-done | bytes 524304
  888.7 107.1 %reduce-scatter.19.cloned.1.call-done = bf16[128,2048]{1,0:T(8,128)(2,1)} async-done(((bf16[2048,2048]{1,0:T(8,128)(2,1)}), bf16[128,2048]{1,0:T(8,128)(2,1)}) %reduce-scatter.19.cloned.1.call-update) | async-done | bytes 524304 | tf_op jit(solution)/shard_map/reduce_scatter | solution.py:688
  999.0 105.1 %reduce-scatter.21.cloned.1.call-done = bf16[128,2048]{1,0:T(8,128)(2,1)} async-done(((bf16[2048,2048]{1,0:T(8,128)(2,1)}), bf16[128,2048]{1,0:T(8,128)(2,1)}) %reduce-scatter.21.cloned.1.call-update) | async-done | bytes 524304 | tf_op jit(solution)/shard_map/reduce_scatter | solution.py:688
  (144 shorter events, 58.1 us)
Async XLA Ops:
  7.2 10.2 copy-start.9
  7.2 10.1 copy-start.14
  7.2 48.7 %all-gather.9.cloned.1.call-start = ((), (), s32[]{:S(2)}) async-start(), calls=%async_computation.8 | async-start | bytes 1671168 | tf_op jit(solution)/shard_map/all_gather | solution.py:630
  13.3 99.7 %all-gather.7.cloned.1.call-start = ((), (), s32[]{:S(2)}) async-start(), calls=%async_computation.7 | async-start | bytes 6291456 | tf_op jit(solution)/shard_map/all_gather | solution.py:640
  14.1 176.1 %all-gather.11.cloned.1.call-start = ((), (), s32[]{:S(2)}) async-start(), calls=%async_computation.9 | async-start | bytes 8912896 | tf_op jit(solution)/shard_map/all_gather | solution.py:630
  14.8 250.6 %all-gather.13.cloned.1.call-start = ((), (), s32[]{:S(2)}) async-start(), calls=%async_computation.10 | async-start | bytes 8912896 | tf_op jit(solution)/shard_map/all_gather | solution.py:630
  15.4 306.5 %all-gather.17.cloned.1.call-start = ((), (), s32[]{:S(2)}) async-start(), calls=%async_computation.13 | async-start | bytes 6291456 | tf_op jit(solution)/shard_map/all_gather | solution.py:644
  16.0 386.0 %all-gather.15.cloned.1.call-start = ((), (), s32[]{:S(2)}) async-start(), calls=%async_computation.11 | async-start | bytes 8912896 | tf_op jit(solution)/shard_map/all_gather | solution.py:630
  16.6 547.0 %reduce-scatter.17.cloned.1.call-start = ((), (), s32[]{:S(2)}) async-start(), calls=%async_computation.15 | async-start | bytes 1572864 | tf_op jit(solution)/shard_map/reduce_scatter | solution.py:703
  113.1 3.4 copy-start.11
  116.5 1.4 copy-start.12
  117.9 2.5 copy-start.8
  119.2 1.3 copy-start.1
  119.2 1.3 copy-start.2
  130.2 1.3 copy-start.3
  190.2 12.6 %copy-start.4 = (f32[4,1024,128]{2,1,0:T(8,128)S(1)}, f32[4,1024,128]{2,1,0:T(8,128)}, u32[]{:S(2)}) copy-start(f32[4,1024,128]{2,1,0:T(8,128)} %copy-done.3) | copy-start | bytes 6291460
  243.4 2.0 copy-start.6
  245.4 2.0 copy-start.7
  428.0 1.6 copy-start.5
  534.5 2.2 copy-start
  544.9 82.6 %reduce-scatter.23.cloned.1.call-start = ((), (), s32[]{:S(2)}) async-start(), calls=%async_computation.19 | async-start | bytes 1671168
  545.2 3.5 copy-start.16
  567.8 115.9 %reduce-scatter.15.cloned.1.call-start = ((), (), s32[]{:S(2)}) async-start(), calls=%async_computation.14 | async-start | bytes 6291456 | tf_op jit(solution)/shard_map/reduce_scatter | solution.py:685
  587.5 233.7 %reduce-scatter.13.cloned.1.call-start = ((), (), s32[]{:S(2)}) async-start(), calls=%async_computation.12 | async-start | bytes 6291456 | tf_op jit(solution)/shard_map/reduce_scatter | solution.py:685
  604.3 0.7 copy-start.15
  604.3 79.4 %copy-start.10 = (bf16[512,2048]{1,0:T(8,128)(2,1)S(1)}, bf16[512,2048]{1,0:T(8,128)(2,1)}, u32[]{:S(2)}) copy-start(bf16[512,2048]{1,0:T(8,128)(2,1)} %param.15) | copy-start | bytes 6291460
  604.3 223.6 %all-reduce.6.cloned.1.call-start = ((), (), s32[]{:S(2)}) async-start(), calls=%async_computation.16 | async-start | bytes 270336 | tf_op jit(solution)/shard_map/psum | solution.py:735
  757.0 130.4 %reduce-scatter.25.cloned.1.call-start = ((), (), s32[]{:S(2)}) async-start(), calls=%async_computation.20 | async-start | bytes 8912896
  786.3 209.5 %reduce-scatter.19.cloned.1.call-start = ((), (), s32[]{:S(2)}) async-start(), calls=%async_computation.17 | async-start | bytes 8912896 | tf_op jit(solution)/shard_map/reduce_scatter | solution.py:688
  800.8 303.3 %reduce-scatter.21.cloned.1.call-start = ((), (), s32[]{:S(2)}) async-start(), calls=%async_computation.18 | async-start | bytes 8912896 | tf_op jit(solution)/shard_map/reduce_scatter | solution.py:688
  815.7 0.9 copy-start.13
Sparse Core Ops, SparseCore 0:
  13.5 42.3 all-gather.8
  57.4 55.6 all-gather.6
  115.2 74.8 all-gather.10
  192.2 73.1 all-gather.12
  266.8 55.0 all-gather.16
  323.9 78.0 all-gather.14
  545.1 18.4 reduce-scatter.16
  567.9 59.5 reduce-scatter.22
  630.4 53.2 reduce-scatter.14
  685.9 54.3 reduce-scatter.12
  757.1 17.8 all-reduce.5
  786.5 100.9 reduce-scatter.24
  891.5 104.3 reduce-scatter.18
  999.8 104.3 reduce-scatter.20
